TPU v7x, 512 devices: a whole 4x4x16 slice. The times are simulated.
512 devices in a mesh: orb: 64 (over x, z), aux: 8 (over y, core).
Axes of the slice: x: 4, y: 4, z: 16, core: 2. Of those that a mesh axis runs over, the one named last changes fastest.
Arguments:
- three_centre: float32 [128, 2, 64, 32768], P('orb', None, None, 'aux'), may hold values from -9 to 9, as said below
- green_occ: float32 [128, 2, 4096], P('orb'), may hold values from -2 to 2, as said below
- green_virt: float32 [128, 2, 4096], P('orb'), may hold values from -2 to 2, as said below
- owned_counts: int32 [64], replicated, may hold values from 1 to 2, 96 in all
- pattern: int32 [128, 3], P('orb'), may hold values 0 or 1
Outputs:
- chi: float32 [512, 512], P('aux', 'orb')
Inputs may be any that keep to these rules, and one draw needn't show every extreme that they name: `owned_counts`: the counts sum to 96. For every row r and auxiliary function P, the diagonal block with entries three_centre[r, 0, k, P * 64 + j] is symmetric in k and j. Every diagonal block green_occ[r, 0] is symmetric. Every diagonal block green_virt[r, 0] is symmetric.
All inputs are finite; a program needn't handle non-finite values. No bound on the sum of `pattern` on one device may be relied on, other than what follows from the above.
Results may differ from a plain program's by a relative error of at most 0.0003.
Values sent between devices are 32-bit elements; how exact they have to be, the bound alone decides.
A program may use at most 128 MiB of HBM per device.

v0:
```python
import jax
import jax.numpy as jnp
from jax import lax
from jax.sharding import PartitionSpec as P

BS = 64


HIGHEST = lax.Precision.HIGHEST


def from_behind(value, axis, steps):
    count = lax.axis_size(axis)
    leading, last = (max(0, -steps), min(count, count - steps))
    return lax.ppermute(value, axis, [(source, source + steps) for source in range(leading, last)])


def flip_blocks(tensor_blocks):
    leading = tensor_blocks.shape[:-2]
    split = tensor_blocks.reshape(leading + (BS, -1, BS))
    return jnp.swapaxes(split, -3, -1).reshape(leading + (BS, -1))


def before_slots(edge_block, local_blocks):
    return jnp.concatenate([edge_block[None], local_blocks[:-1]], axis=0)


def after_slots(edge_block, local_blocks, follows):
    shifted = jnp.concatenate([local_blocks[1:], edge_block[None]], axis=0)
    chosen = follows.reshape((-1,) + (1,) * (local_blocks.ndim - 1))
    return jnp.where(chosen, shifted, edge_block[None])


def squares(flat_blocks):
    return flat_blocks.reshape(flat_blocks.shape[:-1] + (BS, BS))


def flipped(small_blocks):
    return jnp.swapaxes(small_blocks, 1, 2)


def assemble(layout_rows, column_count, slot_count):
    empty_block = jnp.zeros((slot_count, BS, BS), jnp.float32)
    built_rows = []
    for layout_row in layout_rows:
        entries = [empty_block] * column_count
        for column_place, entry_block in layout_row:
            entries[column_place] = entry_block
        built_rows.append(jnp.concatenate(entries, axis=2))
    return jnp.concatenate(built_rows, axis=1)


def local(three_centre, green_occ, green_virt, owned_counts, pattern):
    slot_count = three_centre.shape[0]
    lane_width = three_centre.shape[3]
    aux_local = lane_width // BS
    tensor_flat = BS * lane_width
    green_flat = BS * BS
    orb_index = lax.axis_index("orb")
    block_ends = jnp.cumsum(owned_counts)
    chain_length = block_ends[-1]
    own_count = owned_counts[orb_index]
    first_block = block_ends[orb_index] - own_count
    slot_ids = jnp.arange(slot_count, dtype=jnp.int32)
    slot_valid = slot_ids < own_count
    upper_valid = jnp.logical_and(slot_valid, first_block + slot_ids < chain_length - 1)
    slot_live = slot_valid.astype(jnp.float32)
    pattern_live = (pattern * upper_valid.astype(jnp.int32)[:, None]).astype(jnp.float32)
    diag_b = three_centre[:, 0] * slot_live[:, None, None]
    upper_b = three_centre[:, 1] * pattern_live[:, 0][:, None, None]
    diag_o = green_occ[:, 0] * slot_live[:, None]
    upper_o = green_occ[:, 1] * pattern_live[:, 1][:, None]
    diag_v = green_virt[:, 0] * slot_live[:, None]
    upper_v = green_virt[:, 1] * pattern_live[:, 2][:, None]
    last_slot = own_count - 1
    last_pack = jnp.concatenate(
        [
            diag_b[last_slot].reshape(-1),
            upper_b[last_slot].reshape(-1),
            upper_o[last_slot],
            upper_v[last_slot],
            diag_v[last_slot],
        ],
        axis=0,
    )
    first_pack = jnp.concatenate([diag_b[0].reshape(-1), diag_v[0]], axis=0)
    left_rim = from_behind(last_pack, "orb", 1)
    right_rim = from_behind(first_pack, "orb", -1)
    follows = slot_ids + 1 < own_count
    rim_b = left_rim[:tensor_flat].reshape(BS, lane_width)
    rim_u = left_rim[tensor_flat : 2 * tensor_flat].reshape(BS, lane_width)
    rim_uo = left_rim[2 * tensor_flat : 2 * tensor_flat + green_flat]
    rim_uv = left_rim[2 * tensor_flat + green_flat : 2 * tensor_flat + 2 * green_flat]
    rim_dv = left_rim[2 * tensor_flat + 2 * green_flat :]
    after_b = right_rim[:tensor_flat].reshape(BS, lane_width)
    after_dv = right_rim[tensor_flat:]
    cur_ut = flip_blocks(upper_b)
    prev_b = before_slots(rim_b, diag_b)
    prev_u = before_slots(rim_u, upper_b)
    prev_ut = before_slots(flip_blocks(rim_u), cur_ut)
    next_b = after_slots(after_b, diag_b, follows)
    operands = jnp.concatenate([prev_u, diag_b, cur_ut, prev_b, prev_ut, upper_b, next_b], axis=1)
    cur_do = squares(diag_o)
    cur_uo = squares(upper_o)
    cur_dv = squares(diag_v)
    cur_uv = squares(upper_v)
    prev_uo = squares(before_slots(rim_uo, upper_o))
    prev_uv = squares(before_slots(rim_uv, upper_v))
    prev_dv = squares(before_slots(rim_dv, diag_v))
    next_dv = squares(after_slots(after_dv, diag_v, follows))
    slot_mask = slot_live[:, None, None, None, None]
    occ_grid = assemble(
        [
            [(3, flipped(prev_uo)), (4, cur_do)],
            [(0, flipped(prev_uo)), (1, cur_do), (2, cur_uo)],
            [(5, cur_do), (6, cur_uo)],
        ],
        7,
        slot_count,
    )
    occ_out = jnp.einsum(
        "sxy,syl->sxl", occ_grid, operands, precision=HIGHEST, preferred_element_type=jnp.float32
    )
    occ_split = occ_out.reshape(slot_count, 3, BS, aux_local, BS) * slot_mask
    occ_flat = jnp.transpose(occ_split, (3, 0, 1, 2, 4)).reshape(aux_local, -1)
    virt_grid = assemble(
        [
            [(0, prev_dv), (1, prev_uv)],
            [(0, flipped(prev_uv)), (1, cur_dv), (2, cur_uv)],
            [(1, flipped(cur_uv)), (2, next_dv)],
        ],
        3,
        slot_count,
    )
    virt_out = jnp.einsum(
        "sxy,syl->sxl",
        virt_grid,
        operands[:, : 3 * BS],
        precision=HIGHEST,
        preferred_element_type=jnp.float32,
    )
    virt_split = virt_out.reshape(slot_count, 3, BS, aux_local, BS) * slot_mask
    virt_flat = jnp.transpose(virt_split, (3, 0, 1, 4, 2)).reshape(aux_local, -1)
    occ_cols, virt_cols = (
        lax.all_to_all(occ_flat, "aux", split_axis=1, concat_axis=0, tiled=True),
        lax.all_to_all(virt_flat, "aux", split_axis=1, concat_axis=0, tiled=True),
    )
    norm_scale = lax.rsqrt((3 * chain_length * BS * BS).astype(jnp.float32))
    partial_chi = (
        lax.dot_general(
            occ_cols,
            virt_cols,
            (((1,), (1,)), ((), ())),
            precision=HIGHEST,
            preferred_element_type=jnp.float32,
        )
        * norm_scale
    )
    aux_rows = lax.psum_scatter(partial_chi, "aux", scatter_dimension=0, tiled=True)
    return lax.psum_scatter(aux_rows, "orb", scatter_dimension=1, tiled=True)


def solution(mesh):
    placed = (
        P("orb", None, None, "aux"),
        P("orb", None, None),
        P("orb", None, None),
        P(),
        P("orb", None),
    )
    return jax.shard_map(
        local, mesh=mesh, in_specs=placed, out_specs=P("aux", "orb"), check_vma=False
    )
```

profile of v0, /device:TPU:8, one launch (start us, length us, event | category | flops | bytes accessed | tf_op | source)
XLA Modules:
  0.0 740.1 jit_solution(10810455203807144480)
XLA Ops:
  14.1 2.8 bitcast_multiply_fusion.1
  26.1 5.1 collective-permute-start
  35.8 4.6 squeeze.57
  40.4 5.6 copy.34
  46.0 5.0 multiply_bitcast_fusion.2
  51.0 4.8 reshape.172
  55.8 3.2 slice.163
  58.9 3.0 slice.146
  93.5 3.0 fusion.53
  108.2 4.1 copy.35
  112.3 2.9 broadcast_in_dim_reshape.15
  115.3 3.3 constant_dynamic-update-slice_fusion.2
  128.1 3.5 fusion.8
  131.7 16.5 %fusion.9 = f32[2,192,4096]{2,1,0:T(8,128)} fusion(f32[2,448,4096]{2,1,0:T(8,128)} %fusion.8, f32[2,64,64]{2,1,0:T(8,128)S(1)} %copy-done.13, f32[2,64,64]{2,1,0:T(8,128)S(1)} %copy-done.15, f32[2,64,64]{2,1,0:T(8,128)S(1)} %maximum_bitcast_fusion, f32[192,448]{1,0:T(8,128)S(1)} %pad.34.clone, f32[192,448]{1,0:T(8,128)S(1)} %copy-done.8, ...), kind=kOutput, calls=%fused_computation.23 | convolution fusion | flops 8457437184 | bytes 22446080 | tf_op jit(solution)/shard_map/sxy,syl->sxl/dot_general | solution.py:121
  148.2 10.9 %reshape.173 = f32[2,3,64,64,64]{4,3,2,1,0:T(8,128)} reshape(f32[2,192,4096]{2,1,0:T(8,128)} %fusion.9) | data formatting | bytes 12582912 | tf_op jit(solution)/shard_map/reshape | solution.py:124
  159.1 12.7 %copy.36 = f32[2,3,64,64,64]{2,4,1,0,3:T(8,128)} copy(f32[2,3,64,64,64]{4,3,2,1,0:T(8,128)} %reshape.173) | data formatting | bytes 12582912 | tf_op jit(solution)/shard_map/reshape | solution.py:124
  172.7 8.9 %fusion = f32[2,192,4096]{2,1,0:T(8,128)} fusion(f32[2,64,4096]{2,1,0:T(8,128)} %reshape.172, f32[2,64,4096]{2,1,0:T(8,128)S(1)} %get-tuple-element.14, f32[1,64,4096]{2,1,0:T(8,128)S(1)} %get-tuple-element.26, f32[1,64,4096]{2,1,0:T(8,128)} %broadcast_in_dim_reshape.13, f32[2,64,64]{2,1,0:T(8,128)S(1)} %copy-done.12, f32[2,64,64]{2,1,0:T(8,128)S(1)} %copy-done.11, ...), kind=kOutput, calls=%fused_computation.2 | convolution fusion | flops 3629260800 | bytes 12845056 | tf_op jit(solution)/shard_map/sxy,syl->sxl/dot_general | solution.py:135
  181.6 10.9 %reshape.174 = f32[2,3,64,64,64]{4,3,2,1,0:T(8,128)} reshape(f32[2,192,4096]{2,1,0:T(8,128)} %fusion) | data formatting | bytes 12582912 | tf_op jit(solution)/shard_map/reshape | solution.py:142
  192.4 12.7 %copy.42 = f32[2,3,64,64,64]{2,4,1,0,3:T(8,128)} copy(f32[2,3,64,64,64]{4,3,2,1,0:T(8,128)} %reshape.174) | data formatting | bytes 12582912 | tf_op jit(solution)/shard_map/reshape | solution.py:142
  205.2 20.1 %multiply_bitcast_fusion = (f32[64,2,3,64,64]{4,3,2,1,0:T(8,128)}, f32[64,2,3,64,64]{3,4,2,1,0:T(8,128)}) fusion(f32[2,3,64,64,64]{2,4,1,0,3:T(8,128)} %copy.42, f32[2]{0:T(128)S(1)} %copy-done.21, f32[2,3,64,64,64]{2,4,1,0,3:T(8,128)} %copy.36), kind=kLoop, calls=%fused_computation | loop fusion | flops 3145728 | bytes 25165832 | tf_op jit(solution)/shard_map/transpose | solution.py:143
  225.3 12.6 %copy.37 = f32[64,2,3,64,64]{4,3,2,1,0:T(8,128)} copy(f32[64,2,3,64,64]{3,4,2,1,0:T(8,128)} %get-tuple-element.39) | data formatting | bytes 12582912 | tf_op jit(solution)/shard_map/transpose | solution.py:125
  237.9 10.6 %all_to_all.28 = f32[64,8,3072]{2,1,0:T(8,128)} reshape(f32[64,2,3,64,64]{4,3,2,1,0:T(8,128)} %copy.37) | data formatting | bytes 12582912 | tf_op jit(solution)/shard_map/all_to_all | solution.py:145
  248.5 9.0 %copy.38 = f32[64,8,3072]{2,0,1:T(8,128)} copy(f32[64,8,3072]{2,1,0:T(8,128)} %all_to_all.28) | data formatting | bytes 12582912 | tf_op jit(solution)/shard_map/all_to_all | solution.py:145
  257.5 8.0 %all-to-all-start = ((f32[64,8,3072]{2,0,1:T(8,128)}), f32[64,8,3072]{2,0,1:T(8,128)}, u32[]{:S(2)}, u32[]{:S(2)}) async-start(f32[64,8,3072]{2,0,1:T(8,128)} %copy.38), calls=%async_computation | async-start | bytes 12582912 | tf_op jit(solution)/shard_map/all_to_all | solution.py:145
  265.5 10.6 %all_to_all.32 = f32[64,8,3072]{2,1,0:T(8,128)} reshape(f32[64,2,3,64,64]{4,3,2,1,0:T(8,128)} %get-tuple-element.38) | data formatting | bytes 12582912 | tf_op jit(solution)/shard_map/all_to_all | solution.py:146
  276.1 9.1 %copy.43 = f32[64,8,3072]{2,0,1:T(8,128)} copy(f32[64,8,3072]{2,1,0:T(8,128)} %all_to_all.32) | data formatting | bytes 12582912 | tf_op jit(solution)/shard_map/all_to_all | solution.py:146
  285.2 51.1 %all-to-all-done = f32[64,8,3072]{2,0,1:T(8,128)} async-done(((f32[64,8,3072]{2,0,1:T(8,128)}), f32[64,8,3072]{2,0,1:T(8,128)}, u32[]{:S(2)}, u32[]{:S(2)}) %all-to-all-start) | async-done | bytes 6291488 | tf_op jit(solution)/shard_map/all_to_all | solution.py:145
  336.3 6.1 all-to-all-start.1
  343.1 70.1 %all-to-all-done.1 = f32[64,8,3072]{2,0,1:T(8,128)} async-done(((f32[64,8,3072]{2,0,1:T(8,128)}), f32[64,8,3072]{2,0,1:T(8,128)}, u32[]{:S(2)}, u32[]{:S(2)}) %all-to-all-start.1) | async-done | bytes 6291488 | tf_op jit(solution)/shard_map/all_to_all | solution.py:146
  413.2 14.1 %convolution_multiply_fusion = f32[512,512]{1,0:T(8,128)} fusion(f32[512,3072]{1,0:T(8,128)} %bitcast.15, f32[512,3072]{1,0:T(8,128)} %bitcast.20, f32[]{:T(128)} %bitcast.21), kind=kOutput, calls=%fused_computation.19 | convolution fusion | flops 9663938560 | bytes 13631492 | tf_op jit(solution)/shard_map/dot_general | solution.py:150
  427.4 37.7 %reduce-scatter.3.cloned.1.call-done = f32[64,512]{1,0:T(8,128)} async-done(((f32[512,512]{1,0:T(8,128)}), f32[64,512]{1,0:T(8,128)}) %reduce-scatter.3.cloned.1.call-update) | async-done | bytes 131088 | tf_op jit(solution)/shard_map/reduce_scatter | solution.py:159
  467.1 264.4 %all-reduce.3.cloned.1.call-done = f32[64,512]{1,0:T(8,128)} async-done(((f32[64,512]{1,0:T(8,128)}), f32[64,512]{1,0:T(8,128)}) %all-reduce.3.cloned.1.call-update) | async-done | bytes 131088
  (133 shorter events, 74.5 us)
Async XLA Ops:
  11.8 10.7 %copy-start.20 = (f32[2]{0:T(128)}, f32[2]{0:T(128)S(1)}, u32[]{:S(2)}) copy-start(f32[2]{0:T(128)S(1)} %get-tuple-element.43) | copy-start | bytes 28
  12.8 8.8 %copy-start.23 = (f32[2]{0:T(128)}, f32[2]{0:T(128)S(1)}, u32[]{:S(2)}) copy-start(f32[2]{0:T(128)S(1)} %get-tuple-element.12) | copy-start | bytes 28
  12.8 8.9 %copy-start.22 = (f32[2]{0:T(128)}, f32[2]{0:T(128)S(1)}, u32[]{:S(2)}) copy-start(f32[2]{0:T(128)S(1)} %get-tuple-element.11) | copy-start | bytes 28
  16.9 3.4 copy-start
  19.1 1.5 copy-start.18
  19.1 1.5 copy-start.19
  20.4 13.9 %copy-start.2 = (f32[2,2,64,4096]{3,2,1,0:T(8,128)S(1)}, f32[2,2,64,4096]{3,2,1,0:T(8,128)}, u32[]{:S(2)}) copy-start(f32[2,2,64,4096]{3,2,1,0:T(8,128)} %param.5) | copy-start | bytes 12582916
  26.1 67.4 %collective-permute-start = (f32[536576]{0:T(1024)}, f32[536576]{0:T(1024)}, u32[]{:S(2)}, u32[]{:S(2)}) collective-permute-start(f32[536576]{0:T(1024)} %constant_dynamic-update-slice_fusion.6), channel_id=1, source_target_pairs={{0,8},{8,16},{16,24},{24,32},{32,40},{40,48},{48,56},{56,64},{64,7... | collective-permute-start | bytes 6438920 | tf_op jit(solution)/shard_map/ppermute | solution.py:15
  32.5 50.4 %collective-permute-start.1 = (f32[266240]{0:T(1024)}, f32[266240]{0:T(1024)}, u32[]{:S(2)}, u32[]{:S(2)}) collective-permute-start(f32[266240]{0:T(1024)} %pad_maximum_fusion), channel_id=1, source_target_pairs={{8,0},{16,8},{24,16},{32,24},{40,32},{48,40},{56,48},{64,56},{72,6... | collective-permute-start | bytes 3194888 | tf_op jit(solution)/shard_map/ppermute | solution.py:15
  115.3 3.3 copy-start.5
  115.3 3.3 copy-start.6
  115.3 4.7 copy-start.3
  115.3 4.7 copy-start.4
  118.5 2.9 copy-start.1
  127.2 4.4 copy-start.7
  127.2 4.4 copy-start.8
  127.2 4.4 copy-start.9
  127.2 4.4 copy-start.13
  127.2 4.5 copy-start.15
  159.1 12.7 %copy-start.17 = (f32[4096]{0:T(1024)S(1)}, f32[4096]{0:T(1024)}, u32[]{:S(2)}) copy-start(f32[4096]{0:T(1024)} %get-tuple-element.17) | copy-start | bytes 49156
  159.1 12.8 %copy-start.16 = (f32[1,64,64]{2,1,0:T(8,128)S(1)}, f32[1,64,64]{2,1,0:T(8,128)}, u32[]{:S(2)}) copy-start(f32[1,64,64]{2,1,0:T(8,128)} %concatenate.114) | copy-start | bytes 49156
  159.1 13.6 %copy-start.10 = (f32[2,64,64]{2,1,0:T(8,128)S(1)}, f32[2,64,64]{2,1,0:T(8,128)}, u32[]{:S(2)}) copy-start(f32[2,64,64]{2,1,0:T(8,128)} %copy.41) | copy-start | bytes 98308
  159.1 13.6 %copy-start.11 = (f32[2,64,64]{2,1,0:T(8,128)S(1)}, f32[2,64,64]{2,1,0:T(8,128)}, u32[]{:S(2)}) copy-start(f32[2,64,64]{2,1,0:T(8,128)} %fusion.58) | copy-start | bytes 98308
  159.1 13.6 %copy-start.12 = (f32[2,64,64]{2,1,0:T(8,128)S(1)}, f32[2,64,64]{2,1,0:T(8,128)}, u32[]{:S(2)}) copy-start(f32[2,64,64]{2,1,0:T(8,128)} %maximum_select_fusion.1) | copy-start | bytes 98308
  159.1 13.6 %copy-start.14 = (f32[2,64,64]{2,1,0:T(8,128)S(1)}, f32[2,64,64]{2,1,0:T(8,128)}, u32[]{:S(2)}) copy-start(f32[2,64,64]{2,1,0:T(8,128)} %get-tuple-element.40) | copy-start | bytes 98308
  192.4 12.7 %copy-start.21 = (f32[2]{0:T(128)S(1)}, f32[2]{0:T(128)}, u32[]{:S(2)}) copy-start(f32[2]{0:T(128)} %copy-done.20) | copy-start | bytes 28
  257.5 78.8 %all-to-all-start = ((f32[64,8,3072]{2,0,1:T(8,128)}), f32[64,8,3072]{2,0,1:T(8,128)}, u32[]{:S(2)}, u32[]{:S(2)}) async-start(f32[64,8,3072]{2,0,1:T(8,128)} %copy.38), calls=%async_computation | async-start | bytes 12582912 | tf_op jit(solution)/shard_map/all_to_all | solution.py:145
  336.3 76.9 %all-to-all-start.1 = ((f32[64,8,3072]{2,0,1:T(8,128)}), f32[64,8,3072]{2,0,1:T(8,128)}, u32[]{:S(2)}, u32[]{:S(2)}) async-start(f32[64,8,3072]{2,0,1:T(8,128)} %copy.43), calls=%async_computation.1 | async-start | bytes 12582912 | tf_op jit(solution)/shard_map/all_to_all | solution.py:146
  342.4 122.7 %reduce-scatter.3.cloned.1.call-start = ((), (), s32[]{:S(2)}) async-start(), calls=%async_computation.3 | async-start | bytes 1179648 | tf_op jit(solution)/shard_map/reduce_scatter | solution.py:159
  427.4 304.1 %all-reduce.3.cloned.1.call-start = ((), (), s32[]{:S(2)}) async-start(), calls=%async_computation.4 | async-start | bytes 262144
Sparse Core Ops, SparseCore 0:
  427.5 37.5 reduce-scatter.2
  468.6 262.8 all-reduce.2
where the time goes:
time: 746 us; the launch traced here: 740 us
  waiting for transfers between devices  423 us (57%)
  local copies, waits for them, and re-layouts  188 us (25%)
  other arithmetic  49.6 us (7%)
  matrix products  39.6 us (5%)
  starting transfers between devices  21 us (3%)
  between operations  18.6 us (2%)
    unnamed x3, waiting for transfers between devices  264 us
    all_to_all x1, waiting for transfers between devices, local(): lax.all_to_all(virt_flat, 'aux', split_axis=1, concat_axis=0, tiled=True)  70.1 us
    all_to_all x1, waiting for transfers between devices, local(): lax.all_to_all(occ_flat, 'aux', split_axis=1, concat_axis=0, tiled=True)  51.1 us
    reduce_scatter x1, waiting for transfers between devices, local(): lax.psum_scatter(partial_chi, 'aux', scatter_dimension=0, tiled=True)  37.7 us
    reshape x2, local copies, waits for them, and re-layouts, local(): virt_split = virt_out.reshape(slot_count, 3, BS, aux_local, BS) * slot_mask  23.6 us
    reshape x2, local copies, waits for them, and re-layouts, local(): occ_split = occ_out.reshape(slot_count, 3, BS, aux_local, BS) * slot_mask  23.5 us
    transpose x1, other arithmetic, local(): jnp.transpose(virt_split, (3, 0, 1, 4, 2)).reshape(aux_local, -1)  20.1 us
    all_to_all x2, local copies, waits for them, and re-layouts, local(): lax.all_to_all(virt_flat, 'aux', split_axis=1, concat_axis=0, tiled=True)  19.7 us
  transfers between devices with their start and end apart: 6, of which 4 were waited for; matrix products, arithmetic and copies ran while one was open for 10% of the time, Pallas kernels for 0%

commit v1 on v0

v1 whole, which is shorter than its diff:
```python
import functools
import math

import jax
import jax.numpy as jnp
from jax import lax
from jax.experimental import pallas as pl
from jax.experimental.pallas import tpu as pltpu
from jax.sharding import PartitionSpec as P

BS = 64
NB = 96
NX, NZ = 4, 16
N_ORB = NX * NZ
PAIRS = 8
CP = 2 * PAIRS
CL = CP * BS
NK = 98
HK = NK // 2
MESH = pl.DeviceIdType.MESH
F32, BF16 = jnp.float32, jnp.bfloat16


def split(value):
    high = value.astype(BF16)
    return high, (value - high.astype(F32)).astype(BF16)


def dot3(first, second, dims=(((1,), (0,)), ((), ()))):
    (fh, fl), (sh, sl) = first, second
    dot = functools.partial(lax.dot_general, dimension_numbers=dims, preferred_element_type=F32)
    return dot(fh, sh) + dot(fh, sl) + dot(fl, sh)


def flip(pair):
    turned = pair.T
    return jnp.concatenate([turned[:BS], turned[BS:]], axis=1)


def swap(first, second, left):
    even = jnp.where(left, first, pltpu.roll(second, BS, 1))
    odd = jnp.where(left, pltpu.roll(first, BS, 1), second)
    return even, odd


def twice(block):
    zero = jnp.zeros((BS, BS), F32)
    return jnp.concatenate(
        [jnp.concatenate([block, zero], axis=1), jnp.concatenate([zero, block], axis=1)], axis=0
    )


def kernel(
    scale, tc, go, gv, counts, pattern, out,
    um, lastb, rimp, rimn, gl_s, gl_r, gf_s, gf_r, buf_b, buf_d, got_b, got_d, stage, corner,
    l1, l2, wd, we, chi, rx, zb, rz, fs, rf,
    rim_send, rim_recv, g_send, g_recv, y_send, y_recv, y_local, x_send, x_recv, z_send, z_recv, f_send, f_recv,
):
    chunks = tc.shape[3] // CL
    o, a = lax.axis_index("orb"), lax.axis_index("aux")
    x, z, y, c = o // NZ, o % NZ, a // 2, a % 2
    y1, y3 = y + 1 - 2 * (y % 2), 3 - y
    yd, yb = y1 * (1 - c) + y3 * c, y3 * (1 - c) + y1 * c
    behind, ahead = (o + N_ORB - 1) % N_ORB, (o + 1) % N_ORB

    sources = []
    for cs in range(2):
        kept, other = (y3, y1) if cs == 0 else (y1, y3)
        here = jnp.logical_or(x == y, x == kept)
        ys = jnp.where(here, y, other)
        xs = jnp.where(here, c, 2 + c)
        mine = jnp.logical_and(jnp.logical_and(xs == x, ys == y), c == cs)
        sources.append((xs * NZ + z, ys * 2 + cs, mine))
    yf, cf = jnp.where(x < 2, y, yd), x % 2
    same = jnp.logical_and(yf == y, cf == c)
    targets = [
        (y * NZ + z, yf * 2 + cf, jnp.logical_and(same, x == y)),
        (yb * NZ + z, yf * 2 + cf, jnp.logical_and(same, x == yb)),
    ]

    barrier = pltpu.get_barrier_semaphore()

    def greet(orb, aux):
        pl.semaphore_signal(barrier, inc=1, device_id=(orb, aux), device_id_type=MESH)

    greet(behind, a)
    greet(ahead, a)
    for aux in (y * 2 + 1 - c, y1 * 2, y1 * 2 + 1, y3 * 2, y3 * 2 + 1):
        greet(o, aux)
    for step in range(1, NX):
        greet((x + step) % NX * NZ + z, a)

    @pl.loop(1, NZ)
    def _(step):
        greet(x * NZ + (z + step) % NZ, a)

    for orb, aux, mine in sources:
        pl.when(jnp.logical_not(mine))(functools.partial(greet, orb, aux))

    own = counts[o]
    start = lax.fori_loop(0, N_ORB, lambda i, s: s + jnp.where(i < o, counts[i], 0), jnp.int32(0))
    two = (own > 1).astype(F32)
    one = 1.0 - two
    ok0 = (start < NB - 1).astype(F32)
    ok1 = (start + 1 < NB - 1).astype(F32) * two
    m0 = [pattern[0, i].astype(F32) * ok0 for i in range(3)]
    m1 = [pattern[1, i].astype(F32) * ok1 for i in range(3)]

    uo = [go[0, 1] * m0[1], go[1, 1] * m1[1]]
    uv = [gv[0, 1] * m0[2], gv[1, 1] * m1[2]]
    gl_s[0] = uo[0] * one + uo[1]
    gl_s[1] = uv[0] * one + uv[1]
    gf_s[0] = go[0, 0]
    gf_s[1] = uo[0]
    gf_s[2] = gv[0, 0]

    @pl.loop(0, tc.shape[3] // 512)
    def _(i):
        lanes = pl.ds(pl.multiple_of(i * 512, 512), 512)
        u0, u1 = tc[0, 1, :, lanes] * m0[0], tc[1, 1, :, lanes] * m1[0]
        um[0, :, lanes] = u0
        um[1, :, lanes] = u1
        lastb[0, :, lanes] = tc[0, 0, :, lanes] * one + tc[1, 0, :, lanes] * two
        lastb[1, :, lanes] = u0 * one + u1

    away = [1 - mine.astype(jnp.int32) for _, _, mine in targets]
    pl.semaphore_wait(barrier, 7 + NX - 1 + NZ - 1 + away[0] + away[1])

    def remote(src, dst, send, recv, orb, aux):
        return pltpu.make_async_remote_copy(
            src_ref=src, dst_ref=dst, send_sem=send, recv_sem=recv,
            device_id=(orb, aux), device_id_type=MESH,
        )

    def green_copies():
        return [
            remote(gl_s, gl_r, g_send.at[0], g_recv.at[0], ahead, a),
            remote(gf_s, gf_r, g_send.at[1], g_recv.at[1], behind, a),
        ]

    def rim_copies(ch):
        lanes = pl.ds(pl.multiple_of(ch * CL, CL), CL)
        return [
            remote(lastb.at[:, :, lanes], rimp.at[:, :, lanes], rim_send.at[0, ch], rim_recv.at[0, ch], ahead, a),
            remote(tc.at[0, 0, :, lanes], rimn.at[0, :, lanes], rim_send.at[1, ch], rim_recv.at[1, ch], behind, a),
            remote(um.at[0, :, lanes], rimn.at[1, :, lanes], rim_send.at[2, ch], rim_recv.at[2, ch], behind, a),
        ]

    for copy in green_copies():
        copy.start()

    @pl.loop(0, chunks)
    def _(ch):
        for copy in rim_copies(ch):
            copy.start()

    def y_copies(which, ch):
        buf, got = (buf_b, got_b) if which == 0 else (buf_d, got_d)
        near = [y3, y1] if which == 0 else [y1, y3]
        rows = pl.ds(pl.multiple_of(ch * CP, CP), CP)

        def place(block):
            return pl.ds(pl.multiple_of(block * BS + ch * CP, CP), CP)

        made = [
            remote(
                buf.at[pl.ds((1 - c) * HK, HK), rows], got.at[:, place(c)],
                y_send.at[which, 0, ch], y_recv.at[which, 0, ch], o, y * 2 + 1 - c,
            )
        ]
        for ct in range(2):
            made.append(
                remote(
                    buf.at[pl.ds(ct * HK, HK), rows], got.at[:, place(2 + c)],
                    y_send.at[which, 1 + ct, ch], y_recv.at[which, 1 + c, ch], o, near[ct] * 2 + ct,
                )
            )
        made.append(
            pltpu.make_async_copy(
                buf.at[pl.ds(c * HK, HK), rows], got.at[:, place(c)], y_local.at[which, ch]
            )
        )
        return made

    def y_arrivals(which, ch):
        got = got_b if which == 0 else got_d
        buf = buf_b if which == 0 else buf_d
        rows = pl.ds(pl.multiple_of(ch * CP, CP), CP)
        for j, block in enumerate((1 - c, 2, 3)):
            place = pl.ds(pl.multiple_of(block * BS + ch * CP, CP), CP)
            remote(
                buf.at[pl.ds(0, HK), rows], got.at[:, place],
                y_send.at[which, j, ch], y_recv.at[which, j, ch], o, y * 2 + 1 - c,
            ).wait_recv()

    lane = lax.broadcasted_iota(jnp.int32, (BS // 2, 2 * BS), 1)
    row = lax.broadcasted_iota(jnp.int32, (BS // 2, 2 * BS), 0)
    left = lane < BS
    column = lane % BS
    over, on = column > row, column == row
    far = column == row + BS // 2
    left_row = lax.broadcasted_iota(jnp.int32, (1, 2 * BS), 1) < BS
    half = BS // 2

    def triangle(full, diagonal):
        shifted = pltpu.roll(full[half:], 2 * BS - half, 1)
        packed = jnp.where(over, full[:half], jnp.where(on, diagonal[:half], shifted))
        return packed, jnp.sum(jnp.where(far, diagonal[half:], 0.0), axis=0, keepdims=True)

    def put(buf, ch, edges, fulls, diagonals):
        for p in range(PAIRS):
            even, odd = (slice(2 * p * half, (2 * p + 1) * half), slice((2 * p + 1) * half, (2 * p + 2) * half))
            for s in range(2):
                block = edges[s][p]
                stage[s, even], stage[s, odd] = swap(block[:half], block[half:], left)
            packed, corners = zip(*(triangle(fulls[s][p], diagonals[s][p]) for s in range(2)))
            stage[2, even], stage[2, odd] = swap(packed[0], packed[1], left)
            corner[2 * p : 2 * p + 1], corner[2 * p + 1 : 2 * p + 2] = swap(corners[0], corners[1], left_row)
        rows = pl.ds(pl.multiple_of(ch * CP, CP), CP)
        for kind in range(3):
            for k in range(half):
                buf[kind * half + k, rows] = stage[kind, pl.ds(k, CP, stride=half)]
        buf[3 * half, rows] = corner[...]
        buf[3 * half + 1, rows] = jnp.zeros((CP, 2 * BS), F32)

    def pairs_of(value):
        return [value[:, 2 * BS * p : 2 * BS * (p + 1)] for p in range(PAIRS)]

    @pl.loop(0, chunks)
    def _(ch):
        lanes = pl.ds(pl.multiple_of(ch * CL, CL), CL)
        edges = [pairs_of(um[s, :, lanes]) for s in range(2)]
        diagonals = [pairs_of(tc[0, 0, :, lanes]), pairs_of(tc[1, 0, :, lanes] * two)]
        put(buf_b, ch, edges, diagonals, diagonals)
        for copy in y_copies(0, ch):
            copy.start()

    for copy in green_copies():
        copy.wait()
    do = [None, go[0, 0], go[1, 0] * two + gf_r[0] * one, gf_r[0]]
    uo = [gl_r[0], uo[0], uo[1] + gf_r[1] * one, gf_r[1]]
    dv = [None, gv[0, 0], gv[1, 0] * two + gf_r[2] * one, gf_r[2]]
    uv = [gl_r[1], uv[0], uv[1], None]
    no = jnp.zeros((BS, BS), F32)

    def store(ref, s, value):
        ref[s, 0], ref[s, 1] = split(value)

    def grid(rows):
        return jnp.concatenate([jnp.concatenate(r, axis=1) for r in rows], axis=0)

    for s in range(2):
        n = s + 1
        store(l1, s, grid([
            [uo[n - 1].T, do[n], no, no],
            [uo[n - 1].T, do[n], uo[n], no],
            [uv[n - 1].T, no, no, no],
            [no, dv[n], uv[n], no],
            [no, no, no, uo[n - 1].T],
        ]))
        store(l2, s, grid([
            [do[n], uo[n], no, no],
            [dv[n], uv[n], no, no],
            [dv[n], no, no, no],
            [no, no, uv[n], no],
        ]))
        right = [uv[n - 1], dv[n], uv[n].T, do[n], uo[n].T]
        store(wd, s, jnp.concatenate([twice(r) for r in right], axis=0))
        right = [uv[n], dv[n + 1], uo[n], do[n + 1], uo[n + 1].T]
        store(we, s, jnp.concatenate([twice(r) for r in right], axis=0))

    def stacked(value):
        return jnp.concatenate(pairs_of(value), axis=0)

    @pl.loop(0, chunks)
    def _(ch):
        for copy in rim_copies(ch):
            copy.wait()
        lanes = pl.ds(pl.multiple_of(ch * CL, CL), CL)
        diag = [rimp[0, :, lanes], tc[0, 0, :, lanes],
                tc[1, 0, :, lanes] * two + rimn[0, :, lanes] * one, rimn[0, :, lanes]]
        upper = [rimp[1, :, lanes], um[0, :, lanes],
                 um[1, :, lanes] + rimn[1, :, lanes] * one, rimn[1, :, lanes]]
        edges, fulls, diagonals = [], [], []
        for s in range(2):
            n = s + 1
            turned = jnp.concatenate([flip(b) for b in pairs_of(upper[n])], axis=1)
            s1 = split(jnp.concatenate([upper[n - 1], diag[n], turned, diag[n - 1]], axis=0))
            s2 = split(jnp.concatenate([upper[n], diag[n + 1], upper[n + 1], diag[n]], axis=0))
            t1 = split(dot3((l1[s, 0], l1[s, 1]), s1))
            t2 = split(dot3((l2[s, 0], l2[s, 1]), s2))

            def take(picks):
                return [
                    jnp.concatenate([stacked((t1, t2)[w][part][BS * r : BS * (r + 1)]) for w, r in picks], axis=1)
                    for part in range(2)
                ]

            d = dot3(take([(0, 4), (0, 0), (1, 0), (0, 2), (1, 2)]), (wd[s, 0], wd[s, 1]))
            e = dot3(take([(0, 1), (1, 0), (0, 3), (1, 1), (1, 3)]), (we[s, 0], we[s, 1]))
            d = [d[BS * p : BS * (p + 1)] for p in range(PAIRS)]
            edges.append([e[BS * p : BS * (p + 1)] for p in range(PAIRS)])
            diagonals.append(d)
            fulls.append([b + flip(b) for b in d])
        put(buf_d, ch, edges, fulls, diagonals)
        for copy in y_copies(1, ch):
            copy.start()

    chi[...] = jnp.zeros_like(chi)
    for which in range(2):

        @pl.loop(0, chunks)
        def _(ch):
            y_arrivals(which, ch)
            made = y_copies(which, ch)
            for copy in made[:3]:
                copy.wait_send()
            made[3].wait()

    @pl.loop(0, HK // 7)
    def _(g):
        d = split(jnp.concatenate([got_d[g * 7 + i] for i in range(7)], axis=1))
        b = split(jnp.concatenate([got_b[g * 7 + i] for i in range(7)], axis=1))
        chi[...] += dot3(d, b, (((1,), (1,)), ((), ())))

    def x_copy(step):
        there = (x + step) % NX
        return remote(
            chi.at[pl.ds(pl.multiple_of(there * BS, BS), BS)], rx.at[step - 1],
            x_send.at[step - 1], x_recv.at[step - 1], there * NZ + z, a,
        )

    for step in range(1, NX):
        x_copy(step).start()
    for step in range(1, NX):
        x_copy(step).wait()
    part = chi[pl.ds(pl.multiple_of(x * BS, BS), BS), :] + rx[0] + rx[1] + rx[2]
    turned = part.T
    zb[...] = jnp.concatenate([turned[: 2 * BS], turned[2 * BS :]], axis=1).reshape(NZ, 8, 2 * BS)

    def z_copy(step):
        there = (z + step) % NZ
        return remote(
            zb.at[there], rz.at[step - 1], z_send.at[step - 1], z_recv.at[step - 1], x * NZ + there, a
        )

    @pl.loop(1, NZ)
    def _(step):
        z_copy(step).start()

    @pl.loop(1, NZ)
    def _(step):
        z_copy(step).wait()

    total = zb[z]
    for i in range(NZ - 1):
        total = total + rz[i]
    fs[0] = total
    fs[1] = pltpu.roll(total, BS, 1)

    def f_copy(i):
        orb, aux, _ = targets[i]
        return remote(fs.at[i], rf.at[c], f_send.at[i], f_recv.at[c], orb, aux)

    for i in range(2):
        mine = targets[i][2]

        @pl.when(mine)
        def _():
            rf[c] = fs[i]

        @pl.when(jnp.logical_not(mine))
        def _():
            f_copy(i).start()

    for cs in range(2):

        @pl.when(jnp.logical_not(sources[cs][2]))
        def _():
            remote(fs.at[0], rf.at[cs], f_send.at[0], f_recv.at[cs], o, y * 2 + 1 - c).wait_recv()

    for i in range(2):

        @pl.when(jnp.logical_not(targets[i][2]))
        def _():
            f_copy(i).wait_send()

    out[...] = (rf[0] + rf[1])[:, :BS] * scale


def local(three_centre, green_occ, green_virt, owned_counts, pattern):
    slots, _, _, lanes = three_centre.shape
    chunks = lanes // CL
    aux_local = lanes // BS
    shape = (slots, 2, BS, BS)
    vmem, dma = pltpu.VMEM, pltpu.SemaphoreType.DMA
    smem = pl.BlockSpec(memory_space=pltpu.SMEM)
    block = pl.BlockSpec(memory_space=pltpu.VMEM)
    made = pl.pallas_call(
        functools.partial(kernel, 1.0 / math.sqrt(3 * NB * BS * BS)),
        out_shape=jax.ShapeDtypeStruct((8, BS), F32),
        in_specs=[block, block, block, smem, smem],
        out_specs=block,
        scratch_shapes=[
            vmem((2, BS, lanes), F32),
            vmem((2, BS, lanes), F32),
            vmem((2, BS, lanes), F32),
            vmem((2, BS, lanes), F32),
            vmem((2, BS, BS), F32),
            vmem((2, BS, BS), F32),
            vmem((3, BS, BS), F32),
            vmem((3, BS, BS), F32),
            vmem((NK, aux_local, 2 * BS), F32),
            vmem((NK, aux_local, 2 * BS), F32),
            vmem((HK, 4 * aux_local, 2 * BS), F32),
            vmem((HK, 4 * aux_local, 2 * BS), F32),
            vmem((3, CP * BS // 2, 2 * BS), F32),
            vmem((CP, 2 * BS), F32),
            vmem((2, 2, 5 * BS, 4 * BS), BF16),
            vmem((2, 2, 4 * BS, 4 * BS), BF16),
            vmem((2, 2, 10 * BS, 2 * BS), BF16),
            vmem((2, 2, 10 * BS, 2 * BS), BF16),
            vmem((4 * aux_local, 4 * aux_local), F32),
            vmem((NX - 1, aux_local, 4 * aux_local), F32),
            vmem((NZ, 8, 2 * BS), F32),
            vmem((NZ - 1, 8, 2 * BS), F32),
            vmem((2, 8, 2 * BS), F32),
            vmem((2, 8, 2 * BS), F32),
            dma((3, chunks)),
            dma((3, chunks)),
            dma((2,)),
            dma((2,)),
            dma((2, 3, chunks)),
            dma((2, 3, chunks)),
            dma((2, chunks)),
            dma((NX - 1,)),
            dma((NX - 1,)),
            dma((NZ - 1,)),
            dma((NZ - 1,)),
            dma((2,)),
            dma((2,)),
        ],
        compiler_params=pltpu.CompilerParams(
            collective_id=0, has_side_effects=True, vmem_limit_bytes=56 * 2**20
        ),
    )(
        three_centre,
        green_occ.reshape(shape),
        green_virt.reshape(shape),
        owned_counts,
        pattern,
    )
    return made.T


def solution(mesh):
    placed = (
        P("orb", None, None, "aux"),
        P("orb", None, None),
        P("orb", None, None),
        P(),
        P("orb", None),
    )
    return jax.shard_map(
        local, mesh=mesh, in_specs=placed, out_specs=P("aux", "orb"), check_vma=False
    )
```

time: 746 us -> 116 us (0.16)
  waiting for transfers between devices: 423 us -> 0 us
  local copies, waits for them, and re-layouts: 188 us -> 4.51 us
  Pallas kernels: 0 us -> 112 us
  other arithmetic: 49.6 us -> 0 us
  matrix products: 39.6 us -> 0 us
  starting transfers between devices: 21 us -> 0 us
  between operations: 18.6 us -> 0.01 us
    unnamed x3 -> x0, waiting for transfers between devices: 264 us -> none
    all_to_all x2 -> x0, waiting for transfers between devices: 121 us -> none  [the longest x1 70.1 us: local(): lax.all_to_all(virt_flat, 'aux', split_axis=1, concat_axis=0, tiled=True)]
    pallas_call x0 -> x1, Pallas kernels: none -> 112 us  [local(): pl.pallas_call(functools.partial(kernel, 1.0 / math.sqrt(3 * NB * BS * BS...]
    reshape x6 -> x2, local copies, waits for them, and re-layouts: 52.6 us -> 3.24 us  [the longest x1 1.63 us: local(): green_virt.reshape(shape)]
    dot_general x3 -> x0, matrix products: 39.6 us -> none  [the longest x1 16.5 us: local(): jnp.einsum('sxy,syl->sxl', occ_grid, operands, precision=HIGHEST, preferr...]
    all_to_all x4 -> x0, local copies, waits for them, and re-layouts: 39.3 us -> none  [the longest x2 19.7 us: local(): lax.all_to_all(virt_flat, 'aux', split_axis=1, concat_axis=0, tiled=True)]
    reduce_scatter x1 -> x0, waiting for transfers between devices: 37.7 us -> none  [local(): lax.psum_scatter(partial_chi, 'aux', scatter_dimension=0, tiled=True)]
    transpose x4 -> x0, other arithmetic: 27.6 us -> none  [the longest x1 20.1 us: local(): jnp.transpose(virt_split, (3, 0, 1, 4, 2)).reshape(aux_local, -1)]
  transfers between devices with their start and end apart: 6 -> 0, of which waited for: 4 -> 0; matrix products, arithmetic and copies ran while one was open for 10% -> 0% of each run, Pallas kernels for 0% -> 0%
where the time goes in v1:
time: 116 us
  Pallas kernels  112 us (97%)
  local copies, waits for them, and re-layouts  4.51 us (4%)
    pallas_call x1, Pallas kernels, local(): pl.pallas_call(functools.partial(kernel, 1.0 / math.sqrt(3 * NB * BS * BS...  112 us

profile of v1, /device:TPU:8, one launch (start us, length us, event | category | flops | bytes accessed | tf_op | source)
XLA Modules:
  0.0 116.1 jit_solution(11417583138917511954)
XLA Ops:
  0.0 1.6 %reshape.6.go = f32[2,2,64,64]{3,2,1,0:T(8,128)} reshape(f32[2,2,4096]{2,1,0:T(2,128)} %param.6) | data formatting | bytes 131072 | tf_op jit(solution)/shard_map/reshape | solution.py:448
  1.6 1.6 %reshape.7.gv = f32[2,2,64,64]{3,2,1,0:T(8,128)} reshape(f32[2,2,4096]{2,1,0:T(2,128)} %param.7) | data formatting | bytes 131072 | tf_op jit(solution)/shard_map/reshape | solution.py:449
  3.2 111.5 %shard_map.55 = f32[8,64]{1,0:T(8,128)} custom-call(f32[2,2,64,4096]{3,2,1,0:T(8,128)} %tc.1, f32[2,2,64,64]{3,2,1,0:T(8,128)} %reshape.6.go, f32[2,2,64,64]{3,2,1,0:T(8,128)} %reshape.7.gv, s32[64]{0:T(128)} %counts.1, s32[2,3]{1,0:T(2,128)} %pattern.1), custom_call_target="tpu_custom_call" | custom-call | tf_op jit(solution)/shard_map/pallas_call | solution.py:399
  114.8 1.3 %copy.7 = f32[64,8]{0,1:T(8,128)} copy(f32[64,8]{0,1:T(8,128)} %bitcast.1) | data formatting | bytes 4096

commit v2 on v1

--- a/solution.py
+++ b/solution.py
@@ -51,8 +51,8 @@
 
 
 def kernel(
-    scale, tc, go, gv, counts, pattern, out,
-    um, lastb, rimp, rimn, gl_s, gl_r, gf_s, gf_r, buf_b, buf_d, got_b, got_d, stage, corner,
+    scale, tc, go_rows, gv_rows, counts, pattern, out,
+    go, gv, fold, um, lastb, rimp, rimn, gl_s, gl_r, gf_s, gf_r, buf_b, buf_d, got_b, got_d, stage, corner,
     l1, l2, wd, we, chi, rx, zb, rz, fs, rf,
     rim_send, rim_recv, g_send, g_recv, y_send, y_recv, y_local, x_send, x_recv, z_send, z_recv, f_send, f_recv,
 ):
@@ -106,13 +106,25 @@
     m0 = [pattern[0, i].astype(F32) * ok0 for i in range(3)]
     m1 = [pattern[1, i].astype(F32) * ok1 for i in range(3)]
 
-    uo = [go[0, 1] * m0[1], go[1, 1] * m1[1]]
-    uv = [gv[0, 1] * m0[2], gv[1, 1] * m1[2]]
+    for rows, wide in ((go_rows, go), (gv_rows, gv)):
+        for s in range(2):
+            for kind in range(2):
+                for r in range(BS // 2):
+                    fold[r : r + 1] = rows[s, kind : kind + 1, 2 * BS * r : 2 * BS * (r + 1)]
+                folded = fold[...]
+                wide[s, kind, pl.ds(0, BS // 2, stride=2)] = folded
+                wide[s, kind, pl.ds(1, BS // 2, stride=2)] = pltpu.roll(folded, BS, 1)
+
+    def green(blocks, s, kind):
+        return blocks[s, kind][:, :BS]
+
+    uo = [green(go, 0, 1) * m0[1], green(go, 1, 1) * m1[1]]
+    uv = [green(gv, 0, 1) * m0[2], green(gv, 1, 1) * m1[2]]
     gl_s[0] = uo[0] * one + uo[1]
     gl_s[1] = uv[0] * one + uv[1]
-    gf_s[0] = go[0, 0]
+    gf_s[0] = green(go, 0, 0)
     gf_s[1] = uo[0]
-    gf_s[2] = gv[0, 0]
+    gf_s[2] = green(gv, 0, 0)
 
     @pl.loop(0, tc.shape[3] // 512)
     def _(i):
@@ -123,9 +135,6 @@
         lastb[0, :, lanes] = tc[0, 0, :, lanes] * one + tc[1, 0, :, lanes] * two
         lastb[1, :, lanes] = u0 * one + u1
 
-    away = [1 - mine.astype(jnp.int32) for _, _, mine in targets]
-    pl.semaphore_wait(barrier, 7 + NX - 1 + NZ - 1 + away[0] + away[1])
-
     def remote(src, dst, send, recv, orb, aux):
         return pltpu.make_async_remote_copy(
             src_ref=src, dst_ref=dst, send_sem=send, recv_sem=recv,
@@ -145,14 +154,6 @@
             remote(tc.at[0, 0, :, lanes], rimn.at[0, :, lanes], rim_send.at[1, ch], rim_recv.at[1, ch], behind, a),
             remote(um.at[0, :, lanes], rimn.at[1, :, lanes], rim_send.at[2, ch], rim_recv.at[2, ch], behind, a),
         ]
-
-    for copy in green_copies():
-        copy.start()
-
-    @pl.loop(0, chunks)
-    def _(ch):
-        for copy in rim_copies(ch):
-            copy.start()
 
     def y_copies(which, ch):
         buf, got = (buf_b, got_b) if which == 0 else (buf_d, got_d)
@@ -226,20 +227,38 @@
     def pairs_of(value):
         return [value[:, 2 * BS * p : 2 * BS * (p + 1)] for p in range(PAIRS)]
 
-    @pl.loop(0, chunks)
-    def _(ch):
+    def pack_b(ch):
         lanes = pl.ds(pl.multiple_of(ch * CL, CL), CL)
         edges = [pairs_of(um[s, :, lanes]) for s in range(2)]
         diagonals = [pairs_of(tc[0, 0, :, lanes]), pairs_of(tc[1, 0, :, lanes] * two)]
         put(buf_b, ch, edges, diagonals, diagonals)
+
+    pack_b(0)
+    away = [1 - mine.astype(jnp.int32) for _, _, mine in targets]
+    pl.semaphore_wait(barrier, 7 + NX - 1 + NZ - 1 + away[0] + away[1])
+
+    for copy in y_copies(0, 0):
+        copy.start()
+
+    for copy in green_copies():
+        copy.start()
+
+    @pl.loop(0, chunks)
+    def _(ch):
+        for copy in rim_copies(ch):
+            copy.start()
+
+    @pl.loop(1, chunks)
+    def _(ch):
+        pack_b(ch)
         for copy in y_copies(0, ch):
             copy.start()
 
     for copy in green_copies():
         copy.wait()
-    do = [None, go[0, 0], go[1, 0] * two + gf_r[0] * one, gf_r[0]]
+    do = [None, green(go, 0, 0), green(go, 1, 0) * two + gf_r[0] * one, gf_r[0]]
     uo = [gl_r[0], uo[0], uo[1] + gf_r[1] * one, gf_r[1]]
-    dv = [None, gv[0, 0], gv[1, 0] * two + gf_r[2] * one, gf_r[2]]
+    dv = [None, green(gv, 0, 0), green(gv, 1, 0) * two + gf_r[2] * one, gf_r[2]]
     uv = [gl_r[1], uv[0], uv[1], None]
     no = jnp.zeros((BS, BS), F32)
 
@@ -389,10 +408,9 @@
 
 
 def local(three_centre, green_occ, green_virt, owned_counts, pattern):
-    slots, _, _, lanes = three_centre.shape
+    lanes = three_centre.shape[3]
     chunks = lanes // CL
     aux_local = lanes // BS
-    shape = (slots, 2, BS, BS)
     vmem, dma = pltpu.VMEM, pltpu.SemaphoreType.DMA
     smem = pl.BlockSpec(memory_space=pltpu.SMEM)
     block = pl.BlockSpec(memory_space=pltpu.VMEM)
@@ -402,6 +420,9 @@
         in_specs=[block, block, block, smem, smem],
         out_specs=block,
         scratch_shapes=[
+            vmem((2, 2, BS, 2 * BS), F32),
+            vmem((2, 2, BS, 2 * BS), F32),
+            vmem((BS // 2, 2 * BS), F32),
             vmem((2, BS, lanes), F32),
             vmem((2, BS, lanes), F32),
             vmem((2, BS, lanes), F32),
@@ -445,8 +466,8 @@
         ),
     )(
         three_centre,
-        green_occ.reshape(shape),
-        green_virt.reshape(shape),
+        green_occ,
+        green_virt,
         owned_counts,
         pattern,
     )

time: 116 us -> 112 us (0.966)
  local copies, waits for them, and re-layouts: 4.51 us -> 1.28 us
  Pallas kernels: 112 us -> 110 us
    reshape x2 -> x0, local copies, waits for them, and re-layouts: 3.24 us -> none  [the longest x1 1.63 us: local(): green_virt.reshape(shape)]
where the time goes in v2:
time: 112 us
  Pallas kernels  110 us (98%)
  local copies, waits for them, and re-layouts  1.28 us (1%)
    pallas_call x1, Pallas kernels, local(): pl.pallas_call(functools.partial(kernel, 1.0 / math.sqrt(3 * NB * BS * BS...  110 us

profile of v2, /device:TPU:8, one launch (start us, length us, event | category | flops | bytes accessed | tf_op | source)
XLA Modules:
  0.0 111.7 jit_solution(7125329148138803065)
XLA Ops:
  0.0 110.4 %shard_map.55 = f32[8,64]{1,0:T(8,128)} custom-call(f32[2,2,64,4096]{3,2,1,0:T(8,128)} %tc.1, f32[2,2,4096]{2,1,0:T(2,128)} %go_rows.1, f32[2,2,4096]{2,1,0:T(2,128)} %gv_rows.1, s32[64]{0:T(128)} %counts.1, s32[2,3]{1,0:T(2,128)} %pattern.1), custom_call_target="tpu_custom_call" | custom-call | tf_op jit(solution)/shard_map/pallas_call | solution.py:417
  110.4 1.3 %copy.7 = f32[64,8]{0,1:T(8,128)} copy(f32[64,8]{0,1:T(8,128)} %bitcast.1) | data formatting | bytes 4096

commit v3 on v2

--- a/solution.py
+++ b/solution.py
@@ -52,7 +52,7 @@
 
 def kernel(
     scale, tc, go_rows, gv_rows, counts, pattern, out,
-    go, gv, fold, um, lastb, rimp, rimn, gl_s, gl_r, gf_s, gf_r, buf_b, buf_d, got_b, got_d, stage, corner,
+    go, gv, fold, um, lastb, rimp, rimn, gl_s, gl_r, gf_s, gf_r, buf_b, buf_d, got_b, got_d, stage, corner, high_b, low_b,
     l1, l2, wd, we, chi, rx, zb, rz, fs, rf,
     rim_send, rim_recv, g_send, g_recv, y_send, y_recv, y_local, x_send, x_recv, z_send, z_recv, f_send, f_recv,
 ):
@@ -336,10 +336,16 @@
                 copy.wait_send()
             made[3].wait()
 
+        if which == 0:
+
+            @pl.loop(0, HK)
+            def _(k):
+                high_b[k], low_b[k] = split(got_b[k])
+
     @pl.loop(0, HK // 7)
     def _(g):
         d = split(jnp.concatenate([got_d[g * 7 + i] for i in range(7)], axis=1))
-        b = split(jnp.concatenate([got_b[g * 7 + i] for i in range(7)], axis=1))
+        b = [jnp.concatenate([ref[g * 7 + i] for i in range(7)], axis=1) for ref in (high_b, low_b)]
         chi[...] += dot3(d, b, (((1,), (1,)), ((), ())))
 
     def x_copy(step):
@@ -437,6 +443,8 @@
             vmem((HK, 4 * aux_local, 2 * BS), F32),
             vmem((3, CP * BS // 2, 2 * BS), F32),
             vmem((CP, 2 * BS), F32),
+            vmem((HK, 4 * aux_local, 2 * BS), BF16),
+            vmem((HK, 4 * aux_local, 2 * BS), BF16),
             vmem((2, 2, 5 * BS, 4 * BS), BF16),
             vmem((2, 2, 4 * BS, 4 * BS), BF16),
             vmem((2, 2, 10 * BS, 2 * BS), BF16),

time: 112 us -> 112 us (level)
  no operation moved by 1% of the time
where the time goes in v3:
time: 112 us
  Pallas kernels  111 us (99%)
  local copies, waits for them, and re-layouts  1.28 us (1%)
    pallas_call x1, Pallas kernels, local(): pl.pallas_call(functools.partial(kernel, 1.0 / math.sqrt(3 * NB * BS * BS...  111 us

profile of v3, /device:TPU:8, one launch (start us, length us, event | category | flops | bytes accessed | tf_op | source)
XLA Modules:
  0.0 111.8 jit_solution(3552724463251213575)
XLA Ops:
  0.0 110.6 %shard_map.55 = f32[8,64]{1,0:T(8,128)} custom-call(f32[2,2,64,4096]{3,2,1,0:T(8,128)} %tc.1, f32[2,2,4096]{2,1,0:T(2,128)} %go_rows.1, f32[2,2,4096]{2,1,0:T(2,128)} %gv_rows.1, s32[64]{0:T(128)} %counts.1, s32[2,3]{1,0:T(2,128)} %pattern.1), custom_call_target="tpu_custom_call" | custom-call | tf_op jit(solution)/shard_map/pallas_call | solution.py:423
  110.6 1.3 %copy.7 = f32[64,8]{0,1:T(8,128)} copy(f32[64,8]{0,1:T(8,128)} %bitcast.1) | data formatting | bytes 4096
